TPU v7x, 32 devices: a whole 2x2x4 slice. The times are simulated.
32 devices in a mesh: front: 2 (over core), row: 8 (over z, x), col: 2 (over y).
Axes of the slice: x: 2, y: 2, z: 4, core: 2. Of those that a mesh axis runs over, the one named last changes fastest.
Arguments:
- window: bfloat16 [2, 8192, 1024], P('front', 'row', 'col'), may hold values from -4 to 7.3, as said below
- children: bfloat16 [512, 128, 128], P(('front', 'row', 'col')), may hold values from -4 to 4
- routes: int32 [512, 1], P(('front', 'row', 'col')), may hold values from 0 to 15; in each aligned block of 16 rows (0 to 15, 16 to 31, ...) at most 2 rows name the same one
- slots: int32 [512], P(('front', 'row', 'col')), may hold values from 0 to 15
- pattern: int32 [2, 16, 2], P('front', 'row', 'col'), may hold values 0 or 1
Outputs:
- factored: bfloat16 [2, 8192, 1024], P('front', 'row', 'col')
Inputs may be any that keep to these rules, and one draw needn't show every extreme that they name: `routes`: among the rows of one device (aligned blocks of 16 rows) no owner group is named by more than 2 rows, a bound that some block reaches. `slots`: child blocks land only below the first tile row of each owner's part. `window`: each front's rows and columns [0, 512) hold a symmetric positive definite tile.
All inputs are finite; a program needn't handle non-finite values. No bound on the sum of `pattern` on one device may be relied on, other than what follows from the above.
Results may differ from a plain program's by a relative error of at most 0.0056.
Values may be sent and summed in bfloat16 or wider, within the bound.
A program may use at most 64 MiB of HBM per device.

v0:
```python
import jax
import jax.numpy as jnp
from jax import lax
from jax.sharding import PartitionSpec as P

TILE = 512
SB = 128
CAP = 2


def broadcast(block, axis, holder):
    block = jnp.where(lax.axis_index(axis) == holder, block, jnp.zeros_like(block))
    return lax.psum(block, axis)


def shards(window, children, routes, slots, pattern):
    tile = TILE
    sub = SB
    side = tile // sub
    rows_local = window.shape[1]
    tiles_local = rows_local // tile
    fronts = lax.axis_size("front")
    rows_axis = lax.axis_size("row")
    groups = fronts * rows_axis
    count = children.shape[0]
    buffer_rows = groups * CAP
    target = routes[:, 0]
    labels_grid = lax.broadcasted_iota(jnp.int32, (count, groups), 1)
    hits = (target[:, None] == labels_grid).astype(jnp.int32)
    before = jnp.cumsum(hits, axis=0) - hits
    place = target * CAP + jnp.sum(before * hits, axis=1)
    select = (lax.broadcasted_iota(jnp.int32, (buffer_rows, count), 0) == place[None, :]).astype(
        jnp.bfloat16
    )
    flat = children.reshape(count, sub * sub)
    outgoing = jnp.dot(select, flat, preferred_element_type=jnp.float32).astype(jnp.bfloat16)
    marks = (slots + 1).astype(jnp.bfloat16)
    tagged = jnp.dot(select, marks, preferred_element_type=jnp.float32).astype(jnp.bfloat16)
    incoming, tags = (
        lax.all_to_all(outgoing, ("front", "row"), split_axis=0, concat_axis=0, tiled=True),
        lax.all_to_all(tagged, ("front", "row"), split_axis=0, concat_axis=0, tiled=True),
    )
    slot_count = (tiles_local - 1) * side * side
    slot_marks = (lax.broadcasted_iota(jnp.int32, (slot_count,), 0) + 1).astype(jnp.bfloat16)
    match = (tags[None, :] == slot_marks[:, None]).astype(jnp.bfloat16)
    added = jnp.dot(match, incoming, preferred_element_type=jnp.float32)
    added = (
        added.reshape(tiles_local - 1, side, side, sub, sub)
        .transpose(0, 1, 3, 2, 4)
        .reshape((tiles_local - 1) * tile, tile)
    )
    base = window[0].astype(jnp.float32)
    assembled = jnp.concatenate([base[:tile], base[tile:] + added], axis=0)
    source = broadcast(assembled, "col", 0)
    pivot = broadcast(source[:tile].astype(jnp.bfloat16), "row", 0).astype(jnp.float32)
    factor = jnp.linalg.cholesky(pivot)
    lower = jax.scipy.linalg.solve_triangular(factor, source.T, lower=True).T.astype(jnp.bfloat16)
    column = lax.axis_index("col")
    owner = column // tiles_local
    within = column % tiles_local
    piece = lax.dynamic_slice_in_dim(lower, within * tile, tile, 0)
    partner = broadcast(piece, "row", owner)
    product = lax.dot_general(
        lower, partner, (((1,), (1,)), ((), ())), preferred_element_type=jnp.float32
    )
    live = jnp.repeat(pattern[0, :, 0].astype(jnp.float32), tile)[:, None]
    updated = (assembled - live * product).astype(jnp.bfloat16)
    result = jnp.where(column == 0, lower, updated)
    return result[None]


def solution(mesh):
    placed = (
        P("front", "row", "col"),
        P(("front", "row", "col"), None, None),
        P(("front", "row", "col"), None),
        P(("front", "row", "col")),
        P("front", "row", "col"),
    )
    return jax.shard_map(
        shards, mesh=mesh, in_specs=placed, out_specs=P("front", "row", "col"), check_vma=False
    )
```

profile of v0, /device:TPU:30, one launch (start us, length us, event | category | flops | bytes accessed | tf_op | source)
XLA Modules:
  0.0 427.6 jit_solution(9904782745660950845)
XLA Ops:
  6.5 0.7 fusion.41
  7.3 0.8 select_reduce_fusion.4
  8.1 0.7 multiply_add_fusion
  8.8 0.8 fusion.12
  9.6 0.7 all_to_all.19
  10.3 6.0 %all-to-all-start = ((bf16[16,2,1]{1,2,0:T(2,128)(2,1)}), bf16[16,2,1]{1,2,0:T(2,128)(2,1)S(1)}, u32[]{:S(2)}, u32[]{:S(2)}) async-start(bf16[16,2,1]{1,2,0:T(2,128)(2,1)} %all_to_all.19), calls=%async_computation | async-start | bytes 16384 | tf_op jit(solution)/shard_map/all_to_all | solution.py:41
  16.3 1.5 convolution_convert_fusion
  17.8 1.5 all_to_all.16
  19.3 7.0 %all-to-all-start.1 = ((bf16[16,2,16384]{2,1,0:T(2,128)(2,1)}), bf16[16,2,16384]{2,1,0:T(2,128)(2,1)S(1)}, u32[]{:S(2)}, u32[]{:S(2)}) async-start(bf16[16,2,16384]{2,1,0:T(2,128)(2,1)} %all_to_all.16), calls=%async_computation.1 | async-start | bytes 2097152 | tf_op jit(solution)/shard_map/all_to_all | solution.py:40
  26.3 1.5 convert_element_type.42
  27.8 1.0 slice_bitcast_fusion.1
  29.0 19.9 %all-to-all-done.1 = bf16[16,2,16384]{2,1,0:T(2,128)(2,1)S(1)} async-done(((bf16[16,2,16384]{2,1,0:T(2,128)(2,1)}), bf16[16,2,16384]{2,1,0:T(2,128)(2,1)S(1)}, u32[]{:S(2)}, u32[]{:S(2)}) %all-to-all-start.1) | async-done | bytes 1048608 | tf_op jit(solution)/shard_map/all_to_all | solution.py:40
  49.0 1.2 all_to_all.18
  50.2 1.6 fusion.13
  52.0 1.0 copy-done
  53.0 1.5 fusion
  54.6 63.7 %all-reduce.5.cloned.1.call-done = f32[1024,512]{1,0:T(8,128)} async-done(((f32[1024,512]{1,0:T(8,128)}), f32[1024,512]{1,0:T(8,128)}) %all-reduce.5.cloned.1.call-update) | async-done | bytes 2097168 | tf_op jit(solution)/shard_map/psum | solution.py:13
  118.3 1.3 slice.154
  119.8 0.8 broadcast_select_fusion
  120.9 72.9 %all-reduce.7.cloned.1.call-done = bf16[512,512]{0,1:T(8,128)(2,1)} async-done(((bf16[512,512]{0,1:T(8,128)(2,1)}), bf16[512,512]{0,1:T(8,128)(2,1)}) %all-reduce.7.cloned.1.call-update) | async-done | bytes 524304 | tf_op jit(solution)/shard_map/psum | solution.py:13
  193.8 1.3 copy.22
  195.0 1.2 fusion.18
  196.3 11.7 %cholesky.104 = f32[128,128]{1,0:T(8,128)S(1)} custom-call(f32[128,128]{1,0:T(8,128)S(1)} %cholesky.266), custom_call_target="Cholesky" | custom-call | tf_op jit(solution)/shard_map/jit(cholesky)/cholesky | solution.py:56
  208.0 9.8 %custom-call.31 = f32[1,128,128]{1,2,0:T(8,128)S(1)} custom-call(f32[1,128,128]{2,1,0:T(8,128)S(1)} %get-tuple-element.32), custom_call_target="InvertDiagBlocksLowerTriangular" | custom-call | tf_op jit(solution)/shard_map/jit(cholesky)/cholesky | solution.py:56
  218.6 11.7 %cholesky.217 = f32[128,128]{1,0:T(8,128)S(1)} custom-call(f32[128,128]{1,0:T(8,128)S(1)} %cholesky.270), custom_call_target="Cholesky" | custom-call | tf_op jit(solution)/shard_map/jit(cholesky)/cholesky | solution.py:56
  230.4 10.0 %custom-call.32 = f32[1,128,128]{1,2,0:T(8,128)S(1)} custom-call(f32[1,128,128]{2,1,0:T(8,128)S(1)} %get-tuple-element.29), custom_call_target="InvertDiagBlocksLowerTriangular" | custom-call | tf_op jit(solution)/shard_map/jit(cholesky)/cholesky | solution.py:56
  241.0 11.7 %cholesky.238 = f32[128,128]{1,0:T(8,128)S(1)} custom-call(f32[128,128]{1,0:T(8,128)S(1)} %cholesky.275), custom_call_target="Cholesky" | custom-call | tf_op jit(solution)/shard_map/jit(cholesky)/cholesky | solution.py:56
  252.8 0.7 compare_reduce_fusion.1
  253.4 9.8 %custom-call.33 = f32[1,128,128]{1,2,0:T(8,128)S(1)} custom-call(f32[1,128,128]{2,1,0:T(8,128)S(1)} %get-tuple-element.26), custom_call_target="InvertDiagBlocksLowerTriangular" | custom-call | tf_op jit(solution)/shard_map/jit(cholesky)/cholesky | solution.py:56
  263.9 11.7 %cholesky.255 = f32[128,128]{1,0:T(8,128)S(1)} custom-call(f32[128,128]{1,0:T(8,128)S(1)} %convolution_subtract_fusion.4), custom_call_target="Cholesky" | custom-call | tf_op jit(solution)/shard_map/jit(cholesky)/cholesky | solution.py:56
  275.6 0.7 compare_reduce_fusion
  276.3 0.6 compare_reduce_fusion.2
  279.6 10.6 %while.1 = (s32[]{:T(128)}, f32[512,512]{1,0:T(8,128)S(1)}, s32[4,2]{0,1:T(2,128)S(1)}, f32[4,128,128]{2,1,0:T(8,128)}, s32[]{:T(128)}) while((s32[]{:T(128)}, f32[512,512]{1,0:T(8,128)S(1)}, s32[4,2]{0,1:T(2,128)S(1)}, f32[4,128,128]{2,1,0:T(8,128)}, s32[]{:T(128)}) %tuple.27), condition=%wide.while_cond, body=%wide.while_body.sunk | while | flops 2 | bytes 132705 | solution.py:57
  280.4 2.0 bitcast_dynamic-update-slice_fusion.2
  283.0 2.0 bitcast_dynamic-update-slice_fusion.2
  285.6 2.0 bitcast_dynamic-update-slice_fusion.2
  288.1 2.0 bitcast_dynamic-update-slice_fusion.2
  290.1 40.2 %custom-call.34 = f32[4,128,128]{1,2,0:T(8,128)S(1)} custom-call(f32[4,128,128]{2,1,0:T(8,128)} %get-tuple-element.12), custom_call_target="InvertDiagBlocksLowerTriangular" | custom-call | tf_op jit(solution)/shard_map/jit(_solve_triangular)/triangular_solve | solution.py:57
  330.3 1.8 fusion.21
  332.1 2.0 convolution_subtract_fusion.1
  334.2 0.6 fusion.33
  334.8 2.9 convolution_subtract_fusion
  338.3 3.8 fusion.7
  342.7 1.5 convolution_convert_fusion.1
  344.2 0.7 copy-done.3
  345.0 0.9 select_bitcast_fusion
  346.0 71.6 %all-reduce.9.cloned.1.call-done = bf16[512,512]{1,0:T(8,128)(2,1)} async-done(((bf16[512,512]{1,0:T(8,128)(2,1)}), bf16[512,512]{1,0:T(8,128)(2,1)}) %all-reduce.9.cloned.1.call-update) | async-done | bytes 524304 | tf_op jit(solution)/shard_map/psum | solution.py:13
  417.7 2.9 fusion.11
  (57 shorter events, 7.0 us)
Async XLA Ops:
  10.3 9.0 %all-to-all-start = ((bf16[16,2,1]{1,2,0:T(2,128)(2,1)}), bf16[16,2,1]{1,2,0:T(2,128)(2,1)S(1)}, u32[]{:S(2)}, u32[]{:S(2)}) async-start(bf16[16,2,1]{1,2,0:T(2,128)(2,1)} %all_to_all.19), calls=%async_computation | async-start | bytes 16384 | tf_op jit(solution)/shard_map/all_to_all | solution.py:41
  19.3 29.7 %all-to-all-start.1 = ((bf16[16,2,16384]{2,1,0:T(2,128)(2,1)}), bf16[16,2,16384]{2,1,0:T(2,128)(2,1)S(1)}, u32[]{:S(2)}, u32[]{:S(2)}) async-start(bf16[16,2,16384]{2,1,0:T(2,128)(2,1)} %all_to_all.16), calls=%async_computation.1 | async-start | bytes 2097152 | tf_op jit(solution)/shard_map/all_to_all | solution.py:40
  26.3 92.0 %all-reduce.5.cloned.1.call-start = ((), (), s32[]{:S(2)}) async-start(), calls=%async_computation.2 | async-start | bytes 4194304 | tf_op jit(solution)/shard_map/psum | solution.py:13
  51.8 1.2 copy-start
  54.5 139.3 %all-reduce.7.cloned.1.call-start = ((), (), s32[]{:S(2)}) async-start(), calls=%async_computation.3 | async-start | bytes 1048576 | tf_op jit(solution)/shard_map/psum | solution.py:13
  120.6 297.0 %all-reduce.9.cloned.1.call-start = ((), (), s32[]{:S(2)}) async-start(), calls=%async_computation.4 | async-start | bytes 1048576 | tf_op jit(solution)/shard_map/psum | solution.py:13
  290.1 44.7 %copy-start.2 = (f32[512,512]{1,0:T(8,128)}, f32[512,512]{1,0:T(8,128)S(1)}, u32[]{:S(2)}) copy-start(f32[512,512]{1,0:T(8,128)S(1)} %get-tuple-element.88) | copy-start | bytes 3145732
  330.3 7.4 %copy-start.4 = (f32[4,128,128]{1,2,0:T(8,128)}, f32[4,128,128]{1,2,0:T(8,128)S(1)}, u32[]{:S(2)}) copy-start(f32[4,128,128]{1,2,0:T(8,128)S(1)} %custom-call.34) | copy-start | bytes 786436
  342.7 3.3 copy-start.5
  342.7 75.0 %copy-start.1 = (f32[512,512]{1,0:T(8,128)S(1)}, f32[512,512]{1,0:T(8,128)}, u32[]{:S(2)}) copy-start(f32[512,512]{1,0:T(8,128)} %slice_bitcast_fusion.1) | copy-start | bytes 3145732
  344.2 0.7 copy-start.3
Sparse Core Ops, SparseCore 0:
  54.6 63.5 all-reduce.4
  122.1 71.6 all-reduce.6
  346.1 71.5 all-reduce.8
where the time goes:
time: 435 us; the launch traced here: 428 us
  waiting for transfers between devices  228 us (52%)
  other arithmetic  127 us (29%)
  matrix products  21.9 us (5%)
  local copies, waits for them, and re-layouts  20 us (5%)
  between operations  16.4 us (4%)
  starting transfers between devices  13.3 us (3%)
    psum x3, waiting for transfers between devices, broadcast(): return lax.psum(block, axis)  208 us
    another operation x14, other arithmetic, shards(): factor = jnp.linalg.cholesky(pivot)  78.6 us
    another operation x4, other arithmetic, shards(): jax.scipy.linalg.solve_triangular(factor, source.T, lower=True)  40.4 us
    all_to_all x1, waiting for transfers between devices, shards(): lax.all_to_all(outgoing, ('front', 'row'), split_axis=0, concat_axis=0, t...  19.9 us
    another operation x7, matrix products, shards(): jax.scipy.linalg.solve_triangular(factor, source.T, lower=True)  13.3 us
    another operation x12, local copies, waits for them, and re-layouts  10.3 us
  transfers between devices with their start and end apart: 5, of which 4 were waited for; matrix products, arithmetic and copies ran while one was open for 1% of the time, Pallas kernels for 0%

commit v1 on v0

v1 whole, which is shorter than its diff:
```python
import functools

import jax
import jax.numpy as jnp
from jax import lax
from jax.experimental import pallas as pl
from jax.experimental.pallas import tpu as pltpu
from jax.sharding import PartitionSpec as P

TILE = 512
SB = 128
CAP = 2
SUB = 32
MESH = pl.DeviceIdType.MESH
HIGH = lax.Precision.HIGHEST


def inner_rows(rows):
    inner = 1
    while inner * inner * 4 <= rows:
        inner *= 2
    return inner


def row_tree(f, rel, base, c, rows):
    inner = inner_rows(rows)
    edges = []
    for k in range(1, inner):
        edges.append((rel == 0, (f, lax.rem(base + k, rows), c)))
    edges.append((rel + inner < rows, (f, lax.rem(base + rel + inner, rows), c)))
    return edges


def row_parent(f, rel, base, c, rows):
    inner = inner_rows(rows)
    up = jnp.where(rel < inner, 0, rel - inner)
    return (f, lax.rem(base + up, rows), c)


def remote(src, dst, send, recv, device):
    return pltpu.make_async_remote_copy(
        src_ref=src, dst_ref=dst, send_sem=send, recv_sem=recv, device_id=device, device_id_type=MESH
    )


def exchange_kernel(
    fronts, rows, cols, index, tagrows, children, window, incoming, pivot, top, outgoing,
    send, recv, pivot_send, pivot_recv, top_send, top_recv, local,
):
    f, r, c = lax.axis_index("front"), lax.axis_index("row"), lax.axis_index("col")
    groups = fronts * rows
    me = f * rows + r
    chunk = TILE // 4
    tree = [((r == 0) & (c == 0), (f, 0, k)) for k in range(1, cols)] + row_tree(f, r, 0, c, rows)
    root = (r == 0) & (c == 0)

    barrier = pltpu.get_barrier_semaphore()

    def greet(k, carry):
        g = lax.rem(me + k, groups)
        pl.semaphore_signal(barrier, inc=1, device_id=(g // rows, lax.rem(g, rows), c), device_id_type=MESH)
        return carry

    lax.fori_loop(1, groups, greet, 0)
    for k in range(1, cols):
        pl.semaphore_signal(barrier, inc=1, device_id=(f, r, lax.rem(c + k, cols)), device_id_type=MESH)

    def pack(g, carry):
        for j in range(CAP):
            outgoing[g, j * SB : (j + 1) * SB, :] = children[index[g * CAP + j]]
        outgoing[g, CAP * SB :, :] = tagrows[g]
        return carry

    lax.fori_loop(0, groups, pack, 0)
    pl.semaphore_wait(barrier, groups - 1 + cols - 1)

    def part(ref, i):
        return ref.at[pl.ds(i * chunk, chunk), pl.ds(0, (i + 1) * chunk)]

    def hand_on(i, source):
        for e, (live, device) in enumerate(tree):
            @pl.when(live)
            def _():
                remote(part(source, i), part(pivot, i), pivot_send.at[e, i], pivot_recv.at[i], device).start()

    @pl.when(root)
    def _():
        for i in range(4):
            hand_on(i, window)

    @pl.when(c == 0)
    def _():
        for k in range(1, cols):
            remote(window.at[pl.ds(0, TILE), :], top, top_send.at[k], top_recv, (f, r, k)).start()

    def ship(k):
        g = lax.rem(me + k, groups)
        return remote(outgoing.at[g], incoming.at[me], send.at[k], recv.at[k], (g // rows, lax.rem(g, rows), c))

    def land(k):
        g = lax.rem(me + groups - k, groups)
        return remote(outgoing.at[g], incoming.at[g], send.at[k], recv.at[k], (g // rows, lax.rem(g, rows), c))

    def start(k, carry):
        ship(k).start()
        return carry

    lax.fori_loop(1, groups, start, 0)
    own = pltpu.make_async_copy(outgoing.at[me], incoming.at[me], local.at[0])
    own.start()

    @pl.when(root)
    def _():
        for i in range(4):
            copy = pltpu.make_async_copy(part(window, i), part(pivot, i), local.at[1 + i])
            copy.start()
        for i in range(4):
            pltpu.make_async_copy(part(window, i), part(pivot, i), local.at[1 + i]).wait()

    @pl.when(jnp.logical_not(root))
    def _():
        for i in range(4):
            remote(part(window, i), part(pivot, i), pivot_send.at[0, i], pivot_recv.at[i], (f, 0, 0)).wait_recv()
            hand_on(i, pivot)

    def drain(k, carry):
        land(k).wait_recv()
        ship(k).wait_send()
        return carry

    lax.fori_loop(1, groups, drain, 0)
    own.wait()
    for e, (live, device) in enumerate(tree):
        @pl.when(live)
        def _():
            for i in range(4):
                remote(part(window, i), part(pivot, i), pivot_send.at[e, i], pivot_recv.at[i], device).wait_send()

    @pl.when(c == 0)
    def _():
        for k in range(1, cols):
            remote(window.at[pl.ds(0, TILE), :], top, top_send.at[k], top_recv, (f, r, k)).wait_send()

    @pl.when(c > 0)
    def _():
        remote(window.at[pl.ds(0, TILE), :], top, top_send.at[0], top_recv, (f, r, 0)).wait_recv()


def dot(a, b, dims=(((1,), (0,)), ((), ()))):
    return lax.dot_general(a, b, dims, precision=HIGH, preferred_element_type=jnp.float32)


def invert_small(block):
    row = lax.broadcasted_iota(jnp.int32, (SUB, SB), 0)
    lane = lax.broadcasted_iota(jnp.int32, (SUB, SB), 1)
    work = jnp.where(lane < SUB, block, (lane == row + 2 * SUB).astype(jnp.float32))
    for k in range(SUB):
        column = jnp.broadcast_to(work[:, k : k + 1], (SUB, SB))
        scale = lax.rsqrt(jnp.broadcast_to(column[k : k + 1, :], (SUB, SB)))
        line = jnp.broadcast_to(work[k : k + 1, :], (SUB, SB)) * scale
        work = jnp.where(row > k, work - column * scale * line, jnp.where(row == k, line, work))
    return work[:, 2 * SUB : 3 * SUB]


def factor_block(b, a, u, inv, ext):
    at = b * SB
    width = TILE - at
    ext[:, :width] = a[at : at + SB, at:]
    ext[:, width : width + SB] = (
        lax.broadcasted_iota(jnp.int32, (SB, SB), 0) == lax.broadcasted_iota(jnp.int32, (SB, SB), 1)
    ).astype(jnp.float32)
    steps = SB // SUB
    for s in range(steps):
        lo = s * SUB
        line = ext[lo : lo + SUB, : width + SB]
        diagonal = line[:, :SB]
        if s:
            diagonal = pltpu.roll(diagonal, SB - lo, 1)
        small = invert_small(diagonal)
        new = dot(small, line)
        lane = lax.broadcasted_iota(jnp.int32, new.shape, 1)
        new = jnp.where(lane < lo, 0.0, new)
        ext[lo : lo + SUB, : width + SB] = new
        if s + 1 < steps:
            left = dot(new[:, :SB], new, (((0,), (0,)), ((), ())))
            ext[lo + SUB :, : width + SB] -= left[lo + SUB :]
    u[at : at + SB, at:] = ext[:, :width]
    inv[b] = ext[:, width : width + SB]
    if b < TILE // SB - 1:
        rest = ext[:, SB:width]
        a[at + SB :, at + SB :] -= dot(rest, rest, (((0,), (0,)), ((), ())))


def symmetric(pivot, a):
    for i in range(TILE // SB):
        for j in range(i + 1):
            piece = pivot[i * SB : (i + 1) * SB, j * SB : (j + 1) * SB].astype(jnp.float32)
            a[i * SB : (i + 1) * SB, j * SB : (j + 1) * SB] = piece
            if i > j:
                a[j * SB : (j + 1) * SB, i * SB : (i + 1) * SB] = piece.T


def assemble_kernel(marks, window, incoming, pivot, acc, bottom, u, inv, a, ext):
    groups = incoming.shape[0]
    side = TILE // SB
    acc[...] = window[TILE:, :].astype(jnp.float32)

    def add(p, carry):
        mark = marks[p]

        @pl.when(mark > 0)
        def _():
            slot = mark - 1
            high = pl.ds(pl.multiple_of(slot // side * SB, SB), SB)
            wide = pl.ds(pl.multiple_of(slot % side * SB, SB), SB)
            block = incoming[p // CAP, pl.ds(pl.multiple_of(p % CAP * SB, SB), SB), :]
            acc[high, wide] += block.astype(jnp.float32)

        return carry

    lax.fori_loop(0, groups * CAP, add, 0)
    bottom[...] = acc[...].astype(jnp.bfloat16)
    symmetric(pivot, a)
    u[...] = jnp.zeros_like(u)
    for b in range(TILE // SB):
        factor_block(b, a, u, inv, ext)


def solve_rows(panel, u, inv, out):
    done = []
    for j in range(TILE // SB):
        part = panel[:, j * SB : (j + 1) * SB]
        for k in range(j):
            part = part - dot(done[k], u[k * SB : (k + 1) * SB, j * SB : (j + 1) * SB])
        done.append(dot(part, inv[j], (((1,), (1,)), ((), ()))))
        out[:, j * SB : (j + 1) * SB] = done[-1].astype(jnp.bfloat16)


def finish_kernel(
    rows, cols, pattern, window, top, acc, bottom, u, inv, out, panel, partner, lower, mate,
    panel_send, panel_recv, mate_send, mate_recv,
):
    f, r, c = lax.axis_index("front"), lax.axis_index("row"), lax.axis_index("col")
    tiles = window.shape[0] // TILE
    owner, within = c // tiles, lax.rem(c, tiles)
    rel = lax.rem(r - owner + rows, rows)
    chunk = TILE // 4
    tree = row_tree(f, rel, owner, c, rows)
    parent = row_parent(f, rel, owner, c, rows)

    barrier = pltpu.get_barrier_semaphore()
    for k in range(1, cols):
        pl.semaphore_signal(barrier, inc=1, device_id=(f, r, lax.rem(c + k, cols)), device_id_type=MESH)
    for k in range(1, rows):
        pl.semaphore_signal(barrier, inc=1, device_id=(f, lax.rem(r + k, rows), c), device_id_type=MESH)
    pl.semaphore_wait(barrier, rows - 1 + cols - 1)

    def rows_of(ref, i):
        return ref.at[pl.ds(i * chunk, chunk), :]

    def send_panel(k, i):
        return remote(rows_of(bottom, i), rows_of(panel, i), panel_send.at[k, i], panel_recv.at[i], (f, r, k))

    def give(e, device, source, i):
        return remote(rows_of(source, i), rows_of(partner, i), mate_send.at[e, i], mate_recv.at[i], device)

    def hand_on(source, i):
        for e, (live, device) in enumerate(tree):
            @pl.when(live)
            def _():
                give(e, device, source, i).start()

    @pl.when(c == 0)
    def _():
        for i in range(4):
            for k in range(1, cols):
                send_panel(k, i).start()
        lower[:TILE, :] = window[:TILE, :].astype(jnp.float32)
        lower[TILE:, :] = acc[...]
        solve_rows(lower, u, inv, out)
        for i in range(4):
            for k in range(1, cols):
                send_panel(k, i).wait_send()

    @pl.when(c > 0)
    def _():
        for i in range(4):
            send_panel(0, i).wait_recv()

            @pl.when((rel == 0) & (within != 0))
            def _():
                hand_on(panel, i)
                partner[i * chunk : (i + 1) * chunk, :] = panel[i * chunk : (i + 1) * chunk, :]

            @pl.when((rel == 0) & (within == 0))
            def _():
                hand_on(top, i)
                partner[i * chunk : (i + 1) * chunk, :] = top[i * chunk : (i + 1) * chunk, :]

        lower[:TILE, :] = top[...].astype(jnp.float32)
        lower[TILE:, :] = panel[...].astype(jnp.float32)
        solve_rows(lower, u, inv, out)

        @pl.when(rel > 0)
        def _():
            for i in range(4):
                give(0, parent, partner, i).wait_recv()
                hand_on(partner, i)

        solve_rows(partner[...].astype(jnp.float32), u, inv, mate)
        for t in range(tiles):
            product = lax.dot_general(
                out[t * TILE : (t + 1) * TILE, :], mate[...], (((1,), (1,)), ((), ())),
                preferred_element_type=jnp.float32,
            )
            base = window[:TILE, :].astype(jnp.float32) if t == 0 else acc[(t - 1) * TILE : t * TILE, :]
            live = pattern[t].astype(jnp.float32)
            out[t * TILE : (t + 1) * TILE, :] = (base - live * product).astype(jnp.bfloat16)
        for e, (live, device) in enumerate(tree):
            @pl.when(live)
            def _():
                for i in range(4):
                    give(e, device, partner, i).wait_send()


def spec(space):
    return pl.BlockSpec(memory_space=space)


def shards(window, children, routes, slots, pattern):
    fronts, rows, cols = lax.axis_size("front"), lax.axis_size("row"), lax.axis_size("col")
    groups = fronts * rows
    count = children.shape[0]
    window = window[0]
    height = window.shape[0]
    target = routes[:, 0]
    earlier = (lax.broadcasted_iota(jnp.int32, (count, count), 0) > lax.broadcasted_iota(jnp.int32, (count, count), 1))
    rank = jnp.sum((earlier & (target[:, None] == target[None, :])).astype(jnp.int32), axis=1)
    place = target * CAP + rank
    hit = lax.broadcasted_iota(jnp.int32, (groups * CAP, count), 0) == place[None, :]
    index = jnp.sum(jnp.where(hit, lax.broadcasted_iota(jnp.int32, hit.shape, 1), 0), axis=1)
    tag = jnp.sum(jnp.where(hit, slots[None, :] + 1, 0), axis=1)
    tagrows = jnp.zeros((groups, 16, SB), jnp.float32) + jnp.pad(
        tag.reshape(groups, CAP).astype(jnp.float32), ((0, 0), (0, SB - CAP))
    )[:, None, :]
    tagrows = tagrows.astype(jnp.bfloat16)
    deep = CAP * SB + 16
    edges = cols - 1 + inner_rows(rows)
    vmem, smem, hbm = pltpu.VMEM, pltpu.SMEM, pl.ANY
    dma = pltpu.SemaphoreType.DMA
    incoming, pivot, top = pl.pallas_call(
        functools.partial(exchange_kernel, fronts, rows, cols),
        out_shape=(
            jax.ShapeDtypeStruct((groups, deep, SB), jnp.bfloat16),
            jax.ShapeDtypeStruct((TILE, TILE), jnp.bfloat16),
            jax.ShapeDtypeStruct((TILE, TILE), jnp.bfloat16),
        ),
        in_specs=[spec(smem), spec(vmem), spec(vmem), spec(hbm)],
        out_specs=(spec(hbm), spec(hbm), spec(hbm)),
        scratch_shapes=[
            vmem((groups, deep, SB), jnp.bfloat16),
            dma((groups,)), dma((groups,)), dma((edges, 4)), dma((4,)), dma((cols,)), dma(()), dma((5,)),
        ],
        compiler_params=pltpu.CompilerParams(
            collective_id=0, has_side_effects=True, vmem_limit_bytes=32 << 20
        ),
    )(index, tagrows, children, window)
    marks = incoming[:, CAP * SB, :CAP].astype(jnp.int32).reshape(groups * CAP)
    acc, bottom, u, inv = pl.pallas_call(
        assemble_kernel,
        out_shape=(
            jax.ShapeDtypeStruct((height - TILE, TILE), jnp.float32),
            jax.ShapeDtypeStruct((height - TILE, TILE), jnp.bfloat16),
            jax.ShapeDtypeStruct((TILE, TILE), jnp.float32),
            jax.ShapeDtypeStruct((TILE // SB, SB, SB), jnp.float32),
        ),
        in_specs=[spec(smem), spec(vmem), spec(vmem), spec(vmem)],
        out_specs=(spec(vmem),) * 4,
        scratch_shapes=[vmem((TILE, TILE), jnp.float32), vmem((SB, TILE + SB), jnp.float32)],
        compiler_params=pltpu.CompilerParams(vmem_limit_bytes=48 << 20),
    )(marks, window, incoming, pivot)
    result = pl.pallas_call(
        functools.partial(finish_kernel, rows, cols),
        out_shape=jax.ShapeDtypeStruct((height, TILE), jnp.bfloat16),
        in_specs=[spec(smem)] + [spec(vmem)] * 6,
        out_specs=spec(vmem),
        scratch_shapes=[
            vmem((TILE, TILE), jnp.bfloat16), vmem((TILE, TILE), jnp.bfloat16),
            vmem((height, TILE), jnp.float32), vmem((TILE, TILE), jnp.bfloat16),
            dma((cols, 4)), dma((4,)), dma((inner_rows(rows), 4)), dma((4,)),
        ],
        compiler_params=pltpu.CompilerParams(
            collective_id=1, has_side_effects=True, vmem_limit_bytes=48 << 20
        ),
    )(pattern[0, :, 0], window, top, acc, bottom, u, inv)
    return result[None]


def solution(mesh):
    placed = (
        P("front", "row", "col"),
        P(("front", "row", "col"), None, None),
        P(("front", "row", "col"), None),
        P(("front", "row", "col")),
        P("front", "row", "col"),
    )
    return jax.shard_map(
        shards, mesh=mesh, in_specs=placed, out_specs=P("front", "row", "col"), check_vma=False
    )
```

time: 435 us -> 166 us (0.38); the launches traced: 428 us -> 166 us
  waiting for transfers between devices: 228 us -> 0 us
  Pallas kernels: 0 us -> 161 us
  other arithmetic: 127 us -> 1.72 us
  matrix products: 21.9 us -> 0 us
  local copies, waits for them, and re-layouts: 20 us -> 3.49 us
  between operations: 16.4 us -> 0.08 us
  starting transfers between devices: 13.3 us -> 0 us
    psum x3 -> x0, waiting for transfers between devices: 208 us -> none  [broadcast(): return lax.psum(block, axis)]
    pallas_call x0 -> x3, Pallas kernels: none -> 161 us  [the longest x1 75.4 us: shards(): pl.pallas_call(assemble_kernel, out_shape=(jax.ShapeDtypeStruct((height -...]
    another operation x19 -> x1, other arithmetic: 119 us -> 0.01 us  [the longest x14 78.6 us: shards(): factor = jnp.linalg.cholesky(pivot)]
    all_to_all x2 -> x0, waiting for transfers between devices: 19.9 us -> none  [the longest x1 19.9 us: shards(): lax.all_to_all(outgoing, ('front', 'row'), split_axis=0, concat_axis=0, t...]
    another operation x13 -> x0, matrix products: 15.1 us -> none  [the longest x7 13.3 us: shards(): jax.scipy.linalg.solve_triangular(factor, source.T, lower=True)]
    all_to_all x2 -> x0, starting transfers between devices: 13 us -> none  [the longest x1 6.96 us: shards(): lax.all_to_all(outgoing, ('front', 'row'), split_axis=0, concat_axis=0, t...]
    another operation x20 -> x0, local copies, waits for them, and re-layouts: 10.9 us -> none
    dot_general x4 -> x0, matrix products: 6.81 us -> none  [the longest x1 2.94 us: shards(): lax.dot_general(lower, partner, (((1,), (1,)), ((), ())), preferred_eleme...]
  transfers between devices with their start and end apart: 5 -> 0, of which waited for: 4 -> 0; matrix products, arithmetic and copies ran while one was open for 1% -> 0% of each run, Pallas kernels for 0% -> 0%
where the time goes in v1:
time: 166 us
  Pallas kernels  161 us (97%)
  local copies, waits for them, and re-layouts  3.49 us (2%)
  other arithmetic  1.72 us (1%)
    pallas_call x1, Pallas kernels, shards(): pl.pallas_call(assemble_kernel, out_shape=(jax.ShapeDtypeStruct((height -...  75.4 us
    pallas_call x1, Pallas kernels, shards(): pl.pallas_call(functools.partial(finish_kernel, rows, cols), out_shape=ja...  45.7 us
    pallas_call x1, Pallas kernels, shards(): pl.pallas_call(functools.partial(exchange_kernel, fronts, rows, cols), ou...  39.9 us

profile of v1, /device:TPU:30, one launch (start us, length us, event | category | flops | bytes accessed | tf_op | source)
XLA Modules:
  0.0 166.2 jit_solution(8552226787544172557)
XLA Ops:
  0.0 0.9 convert_reduce_fusion.1
  0.9 0.7 multiply_add_fusion
  1.6 0.1 select_reduce_fusion
  1.7 0.1 convert_element_type.21
  1.8 0.0 copy-start
  1.8 1.2 copy-done
  3.0 0.0 copy-start.2
  3.0 1.0 copy-done.2
  4.1 0.0 copy-start.1
  4.1 39.9 %shard_map.55 = (bf16[16,272,128]{2,1,0:T(8,128)(2,1)S(1)}, bf16[512,512]{1,0:T(8,128)(2,1)S(1)}, bf16[512,512]{1,0:T(8,128)(2,1)S(1)}) custom-call(s32[32]{0:T(128)S(1)} %get-tuple-element.20.index, bf16[16,16,128]{2,1,0:T(8,128)(2,1)S(1)} %add.20.tagrows, bf16[16,128,128]{2,1,0:T(8,128)(2,1)S(1)} %copy-done.2, bf16[1024,512]{1,0:T(8,128)(2,1)S(1)} %bitcast.5), custom_call_target="tpu_custom_call" | custom-call | tf_op jit(solution)/shard_map/pallas_call | solution.py:351
  44.0 0.1 reshape.19.marks
  44.1 0.0 copy-done.1
  44.1 0.0 copy-start.3
  44.1 75.4 %shard_map.56 = (f32[512,512]{1,0:T(8,128)S(1)}, bf16[512,512]{1,0:T(8,128)(2,1)S(1)}, f32[512,512]{1,0:T(8,128)S(1)}, f32[4,128,128]{2,1,0:T(8,128)S(1)}) custom-call(s32[32]{0:T(128)S(1)} %reshape.19.marks, bf16[1024,512]{1,0:T(8,128)(2,1)S(1)} %bitcast.6, bf16[16,272,128]{2,1,0:T(8,128)(2,1)S(1)} %get-tuple-element.13.incoming, ...), custom_call_target="tpu_custom_call" | custom-call | tf_op jit(solution)/shard_map/pallas_call | solution.py:369
  119.5 0.0 copy-done.3
  119.6 45.7 %shard_map.57 = bf16[1024,512]{1,0:T(8,128)(2,1)S(1)} custom-call(s32[2]{0:T(128)S(1)} %bitcast.9, bf16[1024,512]{1,0:T(8,128)(2,1)S(1)} %bitcast.7, bf16[512,512]{1,0:T(8,128)(2,1)S(1)} %get-tuple-element.12.top, f32[512,512]{1,0:T(8,128)S(1)} %get-tuple-element.15.acc, bf16[512,512]{1,0:T(8,128)(2,1)S(1)} %get-tuple-element.16.bottom, ...), custom_call_target="tpu_custom_call" | custom-call | tf_op jit(solution)/shard_map/pallas_call | solution.py:382
  165.2 1.0 copy.7
  (4 shorter events, 0.1 us)
Async XLA Ops:
  1.8 1.2 copy-start
  3.0 1.0 copy-start.2
  4.1 40.0 %copy-start.1 = (bf16[1,1024,512]{2,1,0:T(8,128)(2,1)S(1)}, bf16[1,1024,512]{2,1,0:T(8,128)(2,1)}, u32[]{:S(2)}) copy-start(bf16[1,1024,512]{2,1,0:T(8,128)(2,1)} %param.5) | copy-start | bytes 3145732
  44.1 75.4 %copy-start.3 = (s32[1,2,1]{1,2,0:T(1,128)S(1)}, s32[1,2,1]{1,2,0:T(1,128)}, u32[]{:S(2)}) copy-start(s32[1,2,1]{1,2,0:T(1,128)} %param.9) | copy-start | bytes 28

commit v2 on v1

--- a/solution.py
+++ b/solution.py
@@ -11,6 +11,8 @@
 SB = 128
 CAP = 2
 SUB = 32
+GROUP = 8
+HALF = 2
 MESH = pl.DeviceIdType.MESH
 HIGH = lax.Precision.HIGHEST
 
@@ -44,7 +46,7 @@
 
 
 def exchange_kernel(
-    fronts, rows, cols, index, tagrows, children, window, incoming, pivot, top, outgoing,
+    fronts, rows, cols, index, tagrows, children, window, incoming, top, rest, u, inv, pivot, a, ext, outgoing,
     send, recv, pivot_send, pivot_recv, top_send, top_recv, local,
 ):
     f, r, c = lax.axis_index("front"), lax.axis_index("row"), lax.axis_index("col")
@@ -123,6 +125,11 @@
             remote(part(window, i), part(pivot, i), pivot_send.at[0, i], pivot_recv.at[i], (f, 0, 0)).wait_recv()
             hand_on(i, pivot)
 
+    symmetric(pivot, a)
+    for b in range(HALF):
+        inverse_row(b, factor_block(b, 0, a, u, inv, ext), u, inv)
+    rest[...] = a[HALF * SB :, HALF * SB :]
+
     def drain(k, carry):
         land(k).wait_recv()
         ship(k).wait_send()
@@ -150,45 +157,67 @@
     return lax.dot_general(a, b, dims, precision=HIGH, preferred_element_type=jnp.float32)
 
 
+def down(x, k):
+    return jnp.broadcast_to(x[k : k + 1, :], x.shape)
+
+
 def invert_small(block):
     row = lax.broadcasted_iota(jnp.int32, (SUB, SB), 0)
     lane = lax.broadcasted_iota(jnp.int32, (SUB, SB), 1)
     work = jnp.where(lane < SUB, block, (lane == row + 2 * SUB).astype(jnp.float32))
-    for k in range(SUB):
-        column = jnp.broadcast_to(work[:, k : k + 1], (SUB, SB))
-        scale = lax.rsqrt(jnp.broadcast_to(column[k : k + 1, :], (SUB, SB)))
-        line = jnp.broadcast_to(work[k : k + 1, :], (SUB, SB)) * scale
-        work = jnp.where(row > k, work - column * scale * line, jnp.where(row == k, line, work))
+    pivots = jnp.ones((SUB, SB), jnp.float32)
+    for g in range(0, SUB, GROUP):
+        columns = [jnp.broadcast_to(work[:, g + q : g + q + 1], (SUB, SB)) for q in range(GROUP)]
+        for q in range(GROUP):
+            k = g + q
+            pivot = down(columns[q], k)
+            factor = jnp.where(row > k, columns[q] / pivot, 0.0)
+            pivots = jnp.where(row == k, pivot, pivots)
+            for later in range(q + 1, GROUP):
+                columns[later] = columns[later] - factor * down(columns[later], k)
+            work = work - factor * down(work, k)
+    work = work * lax.rsqrt(pivots)
     return work[:, 2 * SUB : 3 * SUB]
 
 
-def factor_block(b, a, u, inv, ext):
-    at = b * SB
-    width = TILE - at
-    ext[:, :width] = a[at : at + SB, at:]
-    ext[:, width : width + SB] = (
-        lax.broadcasted_iota(jnp.int32, (SB, SB), 0) == lax.broadcasted_iota(jnp.int32, (SB, SB), 1)
-    ).astype(jnp.float32)
+def factor_block(b, first, a, u, inv, ext, hook=None):
+    at = (b - first) * SB
+    here = b * SB
+    row = lax.broadcasted_iota(jnp.int32, (SB, 2 * SB), 0)
+    lane = lax.broadcasted_iota(jnp.int32, (SB, 2 * SB), 1)
+    ext[:, :SB] = a[at : at + SB, at : at + SB]
+    ext[:, SB:] = (row == lane).astype(jnp.float32)[:, :SB]
     steps = SB // SUB
-    for s in range(steps):
-        lo = s * SUB
-        line = ext[lo : lo + SUB, : width + SB]
-        diagonal = line[:, :SB]
-        if s:
-            diagonal = pltpu.roll(diagonal, SB - lo, 1)
-        small = invert_small(diagonal)
+
+    def step(s, carry):
+        if hook is not None:
+            hook(s)
+        lo = pl.multiple_of(s * SUB, SUB)
+        line = ext[pl.ds(lo, SUB), :]
+        small = invert_small(pltpu.roll(line[:, :SB], lax.rem(SB - lo, SB), 1))
         new = dot(small, line)
-        lane = lax.broadcasted_iota(jnp.int32, new.shape, 1)
-        new = jnp.where(lane < lo, 0.0, new)
-        ext[lo : lo + SUB, : width + SB] = new
-        if s + 1 < steps:
-            left = dot(new[:, :SB], new, (((0,), (0,)), ((), ())))
-            ext[lo + SUB :, : width + SB] -= left[lo + SUB :]
-    u[at : at + SB, at:] = ext[:, :width]
-    inv[b] = ext[:, width : width + SB]
-    if b < TILE // SB - 1:
-        rest = ext[:, SB:width]
+        new = jnp.where(lane[:SUB] < lo, 0.0, new)
+        ext[pl.ds(lo, SUB), :] = new
+        left = dot(new[:, :SB], new, (((0,), (0,)), ((), ())))
+        ext[...] -= jnp.where(row >= lo + SUB, left, 0.0)
+        return carry
+
+    lax.fori_loop(0, steps, step, 0)
+    diagonal = ext[:, SB:]
+    if here + SB < TILE:
+        rest = dot(diagonal, a[at : at + SB, at + SB :])
+        u[at : at + SB, here + SB :] = rest
         a[at + SB :, at + SB :] -= dot(rest, rest, (((0,), (0,)), ((), ())))
+    return diagonal
+
+
+def inverse_row(b, diagonal, u, inv):
+    here = b * SB
+    inv[here : here + SB, :] = jnp.zeros((SB, TILE), jnp.float32)
+    inv[here : here + SB, here : here + SB] = diagonal
+    if b:
+        below = dot(u[:here, here : here + SB], inv[:here, :here], (((0,), (0,)), ((), ())))
+        inv[here : here + SB, :here] = -dot(diagonal, below)
 
 
 def symmetric(pivot, a):
@@ -200,7 +229,7 @@
                 a[j * SB : (j + 1) * SB, i * SB : (i + 1) * SB] = piece.T
 
 
-def assemble_kernel(marks, window, incoming, pivot, acc, bottom, u, inv, a, ext):
+def assemble_kernel(marks, window, incoming, acc, bottom):
     groups = incoming.shape[0]
     side = TILE // SB
     acc[...] = window[TILE:, :].astype(jnp.float32)
@@ -220,24 +249,19 @@
 
     lax.fori_loop(0, groups * CAP, add, 0)
     bottom[...] = acc[...].astype(jnp.bfloat16)
-    symmetric(pivot, a)
-    u[...] = jnp.zeros_like(u)
-    for b in range(TILE // SB):
-        factor_block(b, a, u, inv, ext)
-
-
-def solve_rows(panel, u, inv, out):
-    done = []
-    for j in range(TILE // SB):
-        part = panel[:, j * SB : (j + 1) * SB]
-        for k in range(j):
-            part = part - dot(done[k], u[k * SB : (k + 1) * SB, j * SB : (j + 1) * SB])
-        done.append(dot(part, inv[j], (((1,), (1,)), ((), ()))))
-        out[:, j * SB : (j + 1) * SB] = done[-1].astype(jnp.bfloat16)
+
+
+def times(a, b):
+    return lax.dot_general(a, b, (((1,), (1,)), ((), ())), preferred_element_type=jnp.float32)
+
+
+def halves(x):
+    high = x.astype(jnp.bfloat16)
+    return high, (x - high.astype(jnp.float32)).astype(jnp.bfloat16)
 
 
 def finish_kernel(
-    rows, cols, pattern, window, top, acc, bottom, u, inv, out, panel, partner, lower, mate,
+    rows, cols, pattern, window, top, acc, bottom, rest, first_u, first_inv, out, panel, partner, mate, a, u, inv, ext,
     panel_send, panel_recv, mate_send, mate_recv,
 ):
     f, r, c = lax.axis_index("front"), lax.axis_index("row"), lax.axis_index("col")
@@ -270,49 +294,83 @@
             def _():
                 give(e, device, source, i).start()
 
+    inner = inner_rows(rows)
+    depth = jnp.where(rel == 0, 0, 1 + rel // inner)
+    deepest = 1 + (rows - 1) // inner
+
+    def pass_on(h):
+        i = h - 1 - depth
+
+        @pl.when((c > 0) & (i >= 0) & (i < 4))
+        def _():
+            here = pl.ds(pl.multiple_of(i * chunk, chunk), chunk)
+
+            @pl.when(rel == 0)
+            def _():
+                send_panel(0, i).wait_recv()
+
+                @pl.when(within != 0)
+                def _():
+                    partner[here, :] = panel[here, :]
+
+                @pl.when(within == 0)
+                def _():
+                    partner[here, :] = top[here, :]
+
+            @pl.when(rel > 0)
+            def _():
+                give(0, parent, partner, i).wait_recv()
+
+            hand_on(partner, i)
+
     @pl.when(c == 0)
     def _():
         for i in range(4):
             for k in range(1, cols):
                 send_panel(k, i).start()
-        lower[:TILE, :] = window[:TILE, :].astype(jnp.float32)
-        lower[TILE:, :] = acc[...]
-        solve_rows(lower, u, inv, out)
+
+    cut = HALF * SB
+    a[...] = rest[...]
+    u[:cut, :] = first_u[...]
+    inv[:cut, :] = first_inv[...]
+    for b in range(HALF, TILE // SB):
+        base = (b - HALF) * 4
+        low = u.at[cut:, :]
+        diagonal = factor_block(b, HALF, a, low, inv, ext, lambda s: pass_on(base + s))
+        inverse_row(b, diagonal, u, inv)
+    high, low = halves(inv[...])
+
+    @pl.when(c == 0)
+    def _():
+        head = window[:TILE, :]
+        out[:TILE, :] = (times(head, high) + times(head, low)).astype(jnp.bfloat16)
+        for t in range(1, tiles):
+            one, two = halves(acc[(t - 1) * TILE : t * TILE, :])
+            out[t * TILE : (t + 1) * TILE, :] = (
+                times(one, high) + (times(one, low) + times(two, high))
+            ).astype(jnp.bfloat16)
         for i in range(4):
             for k in range(1, cols):
                 send_panel(k, i).wait_send()
 
+    def later(h, carry):
+        pass_on(h)
+        return carry
+
+    lax.fori_loop((TILE // SB - HALF) * 4, deepest + 5, later, 0)
+
     @pl.when(c > 0)
     def _():
-        for i in range(4):
-            send_panel(0, i).wait_recv()
-
-            @pl.when((rel == 0) & (within != 0))
-            def _():
-                hand_on(panel, i)
-                partner[i * chunk : (i + 1) * chunk, :] = panel[i * chunk : (i + 1) * chunk, :]
-
-            @pl.when((rel == 0) & (within == 0))
-            def _():
-                hand_on(top, i)
-                partner[i * chunk : (i + 1) * chunk, :] = top[i * chunk : (i + 1) * chunk, :]
-
-        lower[:TILE, :] = top[...].astype(jnp.float32)
-        lower[TILE:, :] = panel[...].astype(jnp.float32)
-        solve_rows(lower, u, inv, out)
-
         @pl.when(rel > 0)
         def _():
             for i in range(4):
-                give(0, parent, partner, i).wait_recv()
-                hand_on(partner, i)
-
-        solve_rows(partner[...].astype(jnp.float32), u, inv, mate)
+                send_panel(0, i).wait_recv()
+
+        mate[...] = (times(partner[...], high) + times(partner[...], low)).astype(jnp.bfloat16)
         for t in range(tiles):
-            product = lax.dot_general(
-                out[t * TILE : (t + 1) * TILE, :], mate[...], (((1,), (1,)), ((), ())),
-                preferred_element_type=jnp.float32,
-            )
+            source = top[...] if t == 0 else panel[(t - 1) * TILE : t * TILE, :]
+            lower = (times(source, high) + times(source, low)).astype(jnp.bfloat16)
+            product = times(lower, mate[...])
             base = window[:TILE, :].astype(jnp.float32) if t == 0 else acc[(t - 1) * TILE : t * TILE, :]
             live = pattern[t].astype(jnp.float32)
             out[t * TILE : (t + 1) * TILE, :] = (base - live * product).astype(jnp.bfloat16)
@@ -348,51 +406,54 @@
     edges = cols - 1 + inner_rows(rows)
     vmem, smem, hbm = pltpu.VMEM, pltpu.SMEM, pl.ANY
     dma = pltpu.SemaphoreType.DMA
-    incoming, pivot, top = pl.pallas_call(
+    cut = HALF * SB
+    f32, bf16 = jnp.float32, jnp.bfloat16
+    incoming, top, rest, u, inv = pl.pallas_call(
         functools.partial(exchange_kernel, fronts, rows, cols),
         out_shape=(
-            jax.ShapeDtypeStruct((groups, deep, SB), jnp.bfloat16),
-            jax.ShapeDtypeStruct((TILE, TILE), jnp.bfloat16),
-            jax.ShapeDtypeStruct((TILE, TILE), jnp.bfloat16),
+            jax.ShapeDtypeStruct((groups, deep, SB), bf16),
+            jax.ShapeDtypeStruct((TILE, TILE), bf16),
+            jax.ShapeDtypeStruct((TILE - cut, TILE - cut), f32),
+            jax.ShapeDtypeStruct((cut, TILE), f32),
+            jax.ShapeDtypeStruct((cut, TILE), f32),
         ),
         in_specs=[spec(smem), spec(vmem), spec(vmem), spec(hbm)],
-        out_specs=(spec(hbm), spec(hbm), spec(hbm)),
+        out_specs=(spec(hbm), spec(hbm), spec(vmem), spec(vmem), spec(vmem)),
         scratch_shapes=[
-            vmem((groups, deep, SB), jnp.bfloat16),
+            vmem((TILE, TILE), bf16), vmem((TILE, TILE), f32), vmem((SB, 2 * SB), f32),
+            vmem((groups, deep, SB), bf16),
             dma((groups,)), dma((groups,)), dma((edges, 4)), dma((4,)), dma((cols,)), dma(()), dma((5,)),
         ],
         compiler_params=pltpu.CompilerParams(
-            collective_id=0, has_side_effects=True, vmem_limit_bytes=32 << 20
+            collective_id=0, has_side_effects=True, vmem_limit_bytes=40 << 20
         ),
     )(index, tagrows, children, window)
     marks = incoming[:, CAP * SB, :CAP].astype(jnp.int32).reshape(groups * CAP)
-    acc, bottom, u, inv = pl.pallas_call(
+    acc, bottom = pl.pallas_call(
         assemble_kernel,
         out_shape=(
-            jax.ShapeDtypeStruct((height - TILE, TILE), jnp.float32),
-            jax.ShapeDtypeStruct((height - TILE, TILE), jnp.bfloat16),
-            jax.ShapeDtypeStruct((TILE, TILE), jnp.float32),
-            jax.ShapeDtypeStruct((TILE // SB, SB, SB), jnp.float32),
+            jax.ShapeDtypeStruct((height - TILE, TILE), f32),
+            jax.ShapeDtypeStruct((height - TILE, TILE), bf16),
         ),
-        in_specs=[spec(smem), spec(vmem), spec(vmem), spec(vmem)],
-        out_specs=(spec(vmem),) * 4,
-        scratch_shapes=[vmem((TILE, TILE), jnp.float32), vmem((SB, TILE + SB), jnp.float32)],
-        compiler_params=pltpu.CompilerParams(vmem_limit_bytes=48 << 20),
-    )(marks, window, incoming, pivot)
+        in_specs=[spec(smem), spec(vmem), spec(vmem)],
+        out_specs=(spec(vmem),) * 2,
+        compiler_params=pltpu.CompilerParams(vmem_limit_bytes=40 << 20),
+    )(marks, window, incoming)
     result = pl.pallas_call(
         functools.partial(finish_kernel, rows, cols),
-        out_shape=jax.ShapeDtypeStruct((height, TILE), jnp.bfloat16),
-        in_specs=[spec(smem)] + [spec(vmem)] * 6,
+        out_shape=jax.ShapeDtypeStruct((height, TILE), bf16),
+        in_specs=[spec(smem)] + [spec(vmem)] * 7,
         out_specs=spec(vmem),
         scratch_shapes=[
-            vmem((TILE, TILE), jnp.bfloat16), vmem((TILE, TILE), jnp.bfloat16),
-            vmem((height, TILE), jnp.float32), vmem((TILE, TILE), jnp.bfloat16),
+            vmem((TILE, TILE), bf16), vmem((TILE, TILE), bf16), vmem((TILE, TILE), bf16),
+            vmem((TILE - cut, TILE - cut), f32), vmem((TILE, TILE), f32), vmem((TILE, TILE), f32),
+            vmem((SB, 2 * SB), f32),
             dma((cols, 4)), dma((4,)), dma((inner_rows(rows), 4)), dma((4,)),
         ],
         compiler_params=pltpu.CompilerParams(
-            collective_id=1, has_side_effects=True, vmem_limit_bytes=48 << 20
+            collective_id=1, has_side_effects=True, vmem_limit_bytes=40 << 20
         ),
-    )(pattern[0, :, 0], window, top, acc, bottom, u, inv)
+    )(pattern[0, :, 0], window, top, acc, bottom, rest, u, inv)
     return result[None]
 
 

time: 166 us -> 97.1 us (0.58)
  Pallas kernels: 161 us -> 90.9 us
    pallas_call x1, Pallas kernels: 75.4 us -> 1.39 us  [shards(): pl.pallas_call(assemble_kernel, out_shape=(jax.ShapeDtypeStruct((height -...]
    pallas_call x1, Pallas kernels: 39.9 us -> 53.4 us  [shards(): pl.pallas_call(functools.partial(exchange_kernel, fronts, rows, cols), ou...]
    pallas_call x1, Pallas kernels: 45.7 us -> 36.1 us  [shards(): pl.pallas_call(functools.partial(finish_kernel, rows, cols), out_shape=ja...]
    unnamed x9 -> x13, local copies, waits for them, and re-layouts: 3.29 us -> 4.04 us
where the time goes in v2:
time: 97.1 us; the launch traced here: 96.9 us
  Pallas kernels  90.9 us (94%)
  local copies, waits for them, and re-layouts  4.24 us (4%)
  other arithmetic  1.72 us (2%)
    pallas_call x1, Pallas kernels, shards(): pl.pallas_call(functools.partial(exchange_kernel, fronts, rows, cols), ou...  53.4 us
    pallas_call x1, Pallas kernels, shards(): pl.pallas_call(functools.partial(finish_kernel, rows, cols), out_shape=ja...  36.1 us
    unnamed x13, local copies, waits for them, and re-layouts  4.04 us

profile of v2, /device:TPU:30, one launch (start us, length us, event | category | flops | bytes accessed | tf_op | source)
XLA Modules:
  0.0 96.9 jit_solution(9245585171154055996)
XLA Ops:
  0.0 0.9 convert_reduce_fusion.1
  0.9 0.7 multiply_add_fusion
  1.6 0.1 select_reduce_fusion
  1.7 0.1 convert_element_type.21
  1.8 0.0 copy-start
  1.8 1.2 %copy-done = bf16[1,1024,512]{2,1,0:T(8,128)(2,1)S(1)} copy-done((bf16[1,1024,512]{2,1,0:T(8,128)(2,1)S(1)}, bf16[1,1024,512]{2,1,0:T(8,128)(2,1)}, u32[]{:S(2)}) %copy-start) | copy-done | bytes 1048600
  3.0 0.0 copy-start.2
  3.0 1.0 %copy-done.2 = bf16[16,128,128]{2,1,0:T(8,128)(2,1)S(1)} copy-done((bf16[16,128,128]{2,1,0:T(8,128)(2,1)S(1)}, bf16[16,128,128]{2,1,0:T(8,128)(2,1)}, u32[]{:S(2)}) %copy-start.2) | copy-done | bytes 524312
  4.1 0.0 copy-start.1
  4.1 53.4 %shard_map.55 = (bf16[16,272,128]{2,1,0:T(8,128)(2,1)S(1)}, bf16[512,512]{1,0:T(8,128)(2,1)S(1)}, f32[256,256]{1,0:T(8,128)S(1)}, f32[256,512]{1,0:T(8,128)S(1)}, f32[256,512]{1,0:T(8,128)S(1)}) custom-call(s32[32]{0:T(128)S(1)} %get-tuple-element.20.index, bf16[16,16,128]{2,1,0:T(8,128)(2,1)S(1)} %add.20.tagrows, bf16[16,128,128]{2,1,0:T(8,128)(2,1)S(1)} %copy-done.2, ...), custom_call_target="tpu_custom_call" | custom-call | tf_op jit(solution)/shard_map/pallas_call | solution.py:411
  57.5 0.0 copy-start.3
  57.5 0.8 copy-done.3
  58.2 0.0 copy-start.5
  58.3 0.1 reshape.19.marks
  58.4 0.0 copy-done.1
  58.4 0.0 copy-start.4
  58.4 1.4 %shard_map.56 = (f32[512,512]{1,0:T(8,128)S(1)}, bf16[512,512]{1,0:T(8,128)(2,1)S(1)}) custom-call(s32[32]{0:T(128)S(1)} %reshape.19.marks, bf16[1024,512]{1,0:T(8,128)(2,1)S(1)} %bitcast.6, bf16[16,272,128]{2,1,0:T(8,128)(2,1)S(1)} %get-tuple-element.13.incoming), custom_call_target="tpu_custom_call" | custom-call | tf_op jit(solution)/shard_map/pallas_call | solution.py:432
  59.8 0.0 copy-done.5
  59.8 0.0 copy-done.4
  59.8 36.1 %shard_map.57 = bf16[1024,512]{1,0:T(8,128)(2,1)S(1)} custom-call(s32[2]{0:T(128)S(1)} %bitcast.9, bf16[1024,512]{1,0:T(8,128)(2,1)S(1)} %bitcast.7, bf16[512,512]{1,0:T(8,128)(2,1)S(1)} %get-tuple-element.12.top, f32[512,512]{1,0:T(8,128)S(1)} %get-tuple-element.14.acc, bf16[512,512]{1,0:T(8,128)(2,1)S(1)} %get-tuple-element.15.bottom, ...), custom_call_target="tpu_custom_call" | custom-call | tf_op jit(solution)/shard_map/pallas_call | solution.py:442
  95.9 1.0 %copy.7 = bf16[1,1024,512]{2,1,0:T(8,128)(2,1)} copy(bf16[1,1024,512]{2,1,0:T(8,128)(2,1)S(1)} %bitcast.8) | data formatting | bytes 2097152
  (4 shorter events, 0.1 us)
Async XLA Ops:
  1.8 1.2 %copy-start = (bf16[1,1024,512]{2,1,0:T(8,128)(2,1)S(1)}, bf16[1,1024,512]{2,1,0:T(8,128)(2,1)}, u32[]{:S(2)}) copy-start(bf16[1,1024,512]{2,1,0:T(8,128)(2,1)} %param.5) | copy-start | bytes 3145732
  3.0 1.0 %copy-start.2 = (bf16[16,128,128]{2,1,0:T(8,128)(2,1)S(1)}, bf16[16,128,128]{2,1,0:T(8,128)(2,1)}, u32[]{:S(2)}) copy-start(bf16[16,128,128]{2,1,0:T(8,128)(2,1)} %children.1) | copy-start | bytes 1572868
  4.1 54.3 %copy-start.1 = (bf16[1,1024,512]{2,1,0:T(8,128)(2,1)S(1)}, bf16[1,1024,512]{2,1,0:T(8,128)(2,1)}, u32[]{:S(2)}) copy-start(bf16[1,1024,512]{2,1,0:T(8,128)(2,1)} %param.5) | copy-start | bytes 3145732
  57.5 0.8 copy-start.3
  58.2 1.5 %copy-start.5 = (s32[1,2,1]{1,2,0:T(1,128)S(1)}, s32[1,2,1]{1,2,0:T(1,128)}, u32[]{:S(2)}) copy-start(s32[1,2,1]{1,2,0:T(1,128)} %param.9) | copy-start | bytes 28
  58.4 1.4 %copy-start.4 = (f32[256,512]{1,0:T(8,128)S(1)}, f32[256,512]{1,0:T(8,128)}, u32[]{:S(2)}) copy-start(f32[256,512]{1,0:T(8,128)} %copy-done.3) | copy-start | bytes 1572868

commit v3 on v2

--- a/solution.py
+++ b/solution.py
@@ -13,6 +13,7 @@
 SUB = 32
 GROUP = 8
 HALF = 2
+PARTS = 8
 MESH = pl.DeviceIdType.MESH
 HIGH = lax.Precision.HIGHEST
 
@@ -46,16 +47,19 @@
 
 
 def exchange_kernel(
-    fronts, rows, cols, index, tagrows, children, window, incoming, top, rest, u, inv, pivot, a, ext, outgoing,
+    fronts, rows, cols, index, tagrows, children, window, incoming, top, rest, u, inv, pivot, a, ext, held, outgoing,
     send, recv, pivot_send, pivot_recv, top_send, top_recv, local,
 ):
     f, r, c = lax.axis_index("front"), lax.axis_index("row"), lax.axis_index("col")
     groups = fronts * rows
     me = f * rows + r
-    chunk = TILE // 4
+    chunk = TILE // PARTS
+    inner = inner_rows(rows)
     tree = [((r == 0) & (c == 0), (f, 0, k)) for k in range(1, cols)] + row_tree(f, r, 0, c, rows)
     root = (r == 0) & (c == 0)
 
+    fetch = pltpu.make_async_copy(children, held, local.at[PARTS + 1])
+    fetch.start()
     barrier = pltpu.get_barrier_semaphore()
 
     def greet(k, carry):
@@ -67,17 +71,10 @@
     for k in range(1, cols):
         pl.semaphore_signal(barrier, inc=1, device_id=(f, r, lax.rem(c + k, cols)), device_id_type=MESH)
 
-    def pack(g, carry):
-        for j in range(CAP):
-            outgoing[g, j * SB : (j + 1) * SB, :] = children[index[g * CAP + j]]
-        outgoing[g, CAP * SB :, :] = tagrows[g]
-        return carry
-
-    lax.fori_loop(0, groups, pack, 0)
     pl.semaphore_wait(barrier, groups - 1 + cols - 1)
 
     def part(ref, i):
-        return ref.at[pl.ds(i * chunk, chunk), pl.ds(0, (i + 1) * chunk)]
+        return ref.at[pl.ds(i * chunk, chunk), pl.ds(0, (i * chunk // SB + 1) * SB)]
 
     def hand_on(i, source):
         for e, (live, device) in enumerate(tree):
@@ -87,13 +84,18 @@
 
     @pl.when(root)
     def _():
-        for i in range(4):
+        for i in range(PARTS):
             hand_on(i, window)
 
-    @pl.when(c == 0)
-    def _():
-        for k in range(1, cols):
-            remote(window.at[pl.ds(0, TILE), :], top, top_send.at[k], top_recv, (f, r, k)).start()
+    fetch.wait()
+
+    def pack(g, carry):
+        for j in range(CAP):
+            outgoing[g, j * SB : (j + 1) * SB, :] = held[index[g * CAP + j]]
+        outgoing[g, CAP * SB :, :] = tagrows[g]
+        return carry
+
+    lax.fori_loop(0, groups, pack, 0)
 
     def ship(k):
         g = lax.rem(me + k, groups)
@@ -103,27 +105,43 @@
         g = lax.rem(me + groups - k, groups)
         return remote(outgoing.at[g], incoming.at[g], send.at[k], recv.at[k], (g // rows, lax.rem(g, rows), c))
 
-    def start(k, carry):
-        ship(k).start()
-        return carry
-
-    lax.fori_loop(1, groups, start, 0)
+    def start(wanted):
+        def body(k, carry):
+            g = lax.rem(me + k, groups)
+
+            @pl.when(wanted(lax.rem(g, rows) // inner - r // inner))
+            def _():
+                ship(k).start()
+
+            return carry
+
+        lax.fori_loop(1, groups, body, 0)
+
+    start(lambda up: up <= 0)
     own = pltpu.make_async_copy(outgoing.at[me], incoming.at[me], local.at[0])
     own.start()
 
     @pl.when(root)
     def _():
-        for i in range(4):
+        for i in range(PARTS):
             copy = pltpu.make_async_copy(part(window, i), part(pivot, i), local.at[1 + i])
             copy.start()
-        for i in range(4):
+        for i in range(PARTS):
             pltpu.make_async_copy(part(window, i), part(pivot, i), local.at[1 + i]).wait()
 
     @pl.when(jnp.logical_not(root))
     def _():
-        for i in range(4):
+        for i in range(PARTS):
             remote(part(window, i), part(pivot, i), pivot_send.at[0, i], pivot_recv.at[i], (f, 0, 0)).wait_recv()
             hand_on(i, pivot)
+
+    for far in range(1, rows // inner):
+        start(lambda up, far=far: up == far)
+
+    @pl.when(c == 0)
+    def _():
+        for k in range(1, cols):
+            remote(window.at[pl.ds(0, TILE), :], top, top_send.at[k], top_recv, (f, r, k)).start()
 
     symmetric(pivot, a)
     for b in range(HALF):
@@ -140,7 +158,7 @@
     for e, (live, device) in enumerate(tree):
         @pl.when(live)
         def _():
-            for i in range(4):
+            for i in range(PARTS):
                 remote(part(window, i), part(pivot, i), pivot_send.at[e, i], pivot_recv.at[i], device).wait_send()
 
     @pl.when(c == 0)
@@ -261,14 +279,14 @@
 
 
 def finish_kernel(
-    rows, cols, pattern, window, top, acc, bottom, rest, first_u, first_inv, out, panel, partner, mate, a, u, inv, ext,
+    rows, cols, pattern, window, top, acc, bottom, rest, first_u, first_inv, out, panel, partner, mate, lower, a, u, inv, ext,
     panel_send, panel_recv, mate_send, mate_recv,
 ):
     f, r, c = lax.axis_index("front"), lax.axis_index("row"), lax.axis_index("col")
     tiles = window.shape[0] // TILE
     owner, within = c // tiles, lax.rem(c, tiles)
     rel = lax.rem(r - owner + rows, rows)
-    chunk = TILE // 4
+    chunk = TILE // PARTS
     tree = row_tree(f, rel, owner, c, rows)
     parent = row_parent(f, rel, owner, c, rows)
 
@@ -301,7 +319,7 @@
     def pass_on(h):
         i = h - 1 - depth
 
-        @pl.when((c > 0) & (i >= 0) & (i < 4))
+        @pl.when((c > 0) & (i >= 0) & (i < PARTS))
         def _():
             here = pl.ds(pl.multiple_of(i * chunk, chunk), chunk)
 
@@ -325,7 +343,7 @@
 
     @pl.when(c == 0)
     def _():
-        for i in range(4):
+        for i in range(PARTS):
             for k in range(1, cols):
                 send_panel(k, i).start()
 
@@ -349,7 +367,7 @@
             out[t * TILE : (t + 1) * TILE, :] = (
                 times(one, high) + (times(one, low) + times(two, high))
             ).astype(jnp.bfloat16)
-        for i in range(4):
+        for i in range(PARTS):
             for k in range(1, cols):
                 send_panel(k, i).wait_send()
 
@@ -357,27 +375,35 @@
         pass_on(h)
         return carry
 
-    lax.fori_loop((TILE // SB - HALF) * 4, deepest + 5, later, 0)
+    done = (TILE // SB - HALF) * 4
+    lax.fori_loop(done, done + 3, later, 0)
+
+    @pl.when(c > 0)
+    def _():
+        lower[:TILE, :] = (times(top[...], high) + times(top[...], low)).astype(jnp.bfloat16)
+
+    lax.fori_loop(done + 3, max(deepest + PARTS + 1, done + 3), later, 0)
 
     @pl.when(c > 0)
     def _():
         @pl.when(rel > 0)
         def _():
-            for i in range(4):
+            for i in range(PARTS):
                 send_panel(0, i).wait_recv()
 
         mate[...] = (times(partner[...], high) + times(partner[...], low)).astype(jnp.bfloat16)
         for t in range(tiles):
-            source = top[...] if t == 0 else panel[(t - 1) * TILE : t * TILE, :]
-            lower = (times(source, high) + times(source, low)).astype(jnp.bfloat16)
-            product = times(lower, mate[...])
+            if t:
+                source = panel[(t - 1) * TILE : t * TILE, :]
+                lower[t * TILE : (t + 1) * TILE, :] = (times(source, high) + times(source, low)).astype(jnp.bfloat16)
+            product = times(lower[t * TILE : (t + 1) * TILE, :], mate[...])
             base = window[:TILE, :].astype(jnp.float32) if t == 0 else acc[(t - 1) * TILE : t * TILE, :]
             live = pattern[t].astype(jnp.float32)
             out[t * TILE : (t + 1) * TILE, :] = (base - live * product).astype(jnp.bfloat16)
         for e, (live, device) in enumerate(tree):
             @pl.when(live)
             def _():
-                for i in range(4):
+                for i in range(PARTS):
                     give(e, device, partner, i).wait_send()
 
 
@@ -417,12 +443,12 @@
             jax.ShapeDtypeStruct((cut, TILE), f32),
             jax.ShapeDtypeStruct((cut, TILE), f32),
         ),
-        in_specs=[spec(smem), spec(vmem), spec(vmem), spec(hbm)],
+        in_specs=[spec(smem), spec(vmem), spec(hbm), spec(hbm)],
         out_specs=(spec(hbm), spec(hbm), spec(vmem), spec(vmem), spec(vmem)),
         scratch_shapes=[
             vmem((TILE, TILE), bf16), vmem((TILE, TILE), f32), vmem((SB, 2 * SB), f32),
-            vmem((groups, deep, SB), bf16),
-            dma((groups,)), dma((groups,)), dma((edges, 4)), dma((4,)), dma((cols,)), dma(()), dma((5,)),
+            vmem((count, SB, SB), bf16), vmem((groups, deep, SB), bf16),
+            dma((groups,)), dma((groups,)), dma((edges, PARTS)), dma((PARTS,)), dma((cols,)), dma(()), dma((PARTS + 2,)),
         ],
         compiler_params=pltpu.CompilerParams(
             collective_id=0, has_side_effects=True, vmem_limit_bytes=40 << 20
@@ -445,10 +471,10 @@
         in_specs=[spec(smem)] + [spec(vmem)] * 7,
         out_specs=spec(vmem),
         scratch_shapes=[
-            vmem((TILE, TILE), bf16), vmem((TILE, TILE), bf16), vmem((TILE, TILE), bf16),
+            vmem((TILE, TILE), bf16), vmem((TILE, TILE), bf16), vmem((TILE, TILE), bf16), vmem((height, TILE), bf16),
             vmem((TILE - cut, TILE - cut), f32), vmem((TILE, TILE), f32), vmem((TILE, TILE), f32),
             vmem((SB, 2 * SB), f32),
-            dma((cols, 4)), dma((4,)), dma((inner_rows(rows), 4)), dma((4,)),
+            dma((cols, PARTS)), dma((PARTS,)), dma((inner_rows(rows), PARTS)), dma((PARTS,)),
         ],
         compiler_params=pltpu.CompilerParams(
             collective_id=1, has_side_effects=True, vmem_limit_bytes=40 << 20

time: 97.1 us -> 93.1 us (0.959)
  Pallas kernels: 90.9 us -> 86.8 us
    pallas_call x1, Pallas kernels: 36.1 us -> 32.6 us  [shards(): pl.pallas_call(functools.partial(finish_kernel, rows, cols), out_shape=ja...]
where the time goes in v3:
time: 93.1 us; the launch traced here: 92.8 us
  Pallas kernels  86.8 us (93%)
  local copies, waits for them, and re-layouts  4.24 us (5%)
  other arithmetic  1.72 us (2%)
    pallas_call x1, Pallas kernels, shards(): pl.pallas_call(functools.partial(exchange_kernel, fronts, rows, cols), ou...  52.5 us
    pallas_call x1, Pallas kernels, shards(): pl.pallas_call(functools.partial(finish_kernel, rows, cols), out_shape=ja...  32.6 us
    unnamed x13, local copies, waits for them, and re-layouts  4.04 us

profile of v3, /device:TPU:30, one launch (start us, length us, event | category | flops | bytes accessed | tf_op | source)
XLA Modules:
  0.0 92.8 jit_solution(12080840019855883205)
XLA Ops:
  0.0 0.9 convert_reduce_fusion.1
  0.9 0.7 multiply_add_fusion
  1.6 0.1 select_reduce_fusion
  1.7 0.1 convert_element_type.21
  1.8 0.0 copy-start
  1.8 1.2 %copy-done = bf16[1,1024,512]{2,1,0:T(8,128)(2,1)S(1)} copy-done((bf16[1,1024,512]{2,1,0:T(8,128)(2,1)S(1)}, bf16[1,1024,512]{2,1,0:T(8,128)(2,1)}, u32[]{:S(2)}) %copy-start) | copy-done | bytes 1048600
  3.0 0.0 copy-start.2
  3.0 1.0 %copy-done.2 = bf16[16,128,128]{2,1,0:T(8,128)(2,1)S(1)} copy-done((bf16[16,128,128]{2,1,0:T(8,128)(2,1)S(1)}, bf16[16,128,128]{2,1,0:T(8,128)(2,1)}, u32[]{:S(2)}) %copy-start.2) | copy-done | bytes 524312
  4.1 0.0 copy-start.1
  4.1 52.5 %shard_map.55 = (bf16[16,272,128]{2,1,0:T(8,128)(2,1)S(1)}, bf16[512,512]{1,0:T(8,128)(2,1)S(1)}, f32[256,256]{1,0:T(8,128)S(1)}, f32[256,512]{1,0:T(8,128)S(1)}, f32[256,512]{1,0:T(8,128)S(1)}) custom-call(s32[32]{0:T(128)S(1)} %get-tuple-element.20.index, bf16[16,16,128]{2,1,0:T(8,128)(2,1)S(1)} %add.20.tagrows, bf16[16,128,128]{2,1,0:T(8,128)(2,1)S(1)} %copy-done.2, ...), custom_call_target="tpu_custom_call" | custom-call | tf_op jit(solution)/shard_map/pallas_call | solution.py:437
  56.6 0.0 copy-start.3
  56.6 0.8 copy-done.3
  57.4 0.0 copy-start.5
  57.4 0.1 reshape.19.marks
  57.5 0.0 copy-done.1
  57.5 0.0 copy-start.4
  57.5 1.8 %shard_map.56 = (f32[512,512]{1,0:T(8,128)S(1)}, bf16[512,512]{1,0:T(8,128)(2,1)S(1)}) custom-call(s32[32]{0:T(128)S(1)} %reshape.19.marks, bf16[1024,512]{1,0:T(8,128)(2,1)S(1)} %bitcast.6, bf16[16,272,128]{2,1,0:T(8,128)(2,1)S(1)} %get-tuple-element.13.incoming), custom_call_target="tpu_custom_call" | custom-call | tf_op jit(solution)/shard_map/pallas_call | solution.py:458
  59.3 0.0 copy-done.5
  59.3 0.0 copy-done.4
  59.3 32.6 %shard_map.57 = bf16[1024,512]{1,0:T(8,128)(2,1)S(1)} custom-call(s32[2]{0:T(128)S(1)} %bitcast.9, bf16[1024,512]{1,0:T(8,128)(2,1)S(1)} %bitcast.7, bf16[512,512]{1,0:T(8,128)(2,1)S(1)} %get-tuple-element.12.top, f32[512,512]{1,0:T(8,128)S(1)} %get-tuple-element.14.acc, bf16[512,512]{1,0:T(8,128)(2,1)S(1)} %get-tuple-element.15.bottom, ...), custom_call_target="tpu_custom_call" | custom-call | tf_op jit(solution)/shard_map/pallas_call | solution.py:468
  91.9 1.0 %copy.7 = bf16[1,1024,512]{2,1,0:T(8,128)(2,1)} copy(bf16[1,1024,512]{2,1,0:T(8,128)(2,1)S(1)} %bitcast.8) | data formatting | bytes 2097152
  (4 shorter events, 0.1 us)
Async XLA Ops:
  1.8 1.2 %copy-start = (bf16[1,1024,512]{2,1,0:T(8,128)(2,1)S(1)}, bf16[1,1024,512]{2,1,0:T(8,128)(2,1)}, u32[]{:S(2)}) copy-start(bf16[1,1024,512]{2,1,0:T(8,128)(2,1)} %param.5) | copy-start | bytes 3145732
  3.0 1.0 %copy-start.2 = (bf16[16,128,128]{2,1,0:T(8,128)(2,1)S(1)}, bf16[16,128,128]{2,1,0:T(8,128)(2,1)}, u32[]{:S(2)}) copy-start(bf16[16,128,128]{2,1,0:T(8,128)(2,1)} %children.1) | copy-start | bytes 1572868
  4.1 53.4 %copy-start.1 = (bf16[1,1024,512]{2,1,0:T(8,128)(2,1)S(1)}, bf16[1,1024,512]{2,1,0:T(8,128)(2,1)}, u32[]{:S(2)}) copy-start(bf16[1,1024,512]{2,1,0:T(8,128)(2,1)} %param.5) | copy-start | bytes 3145732
  56.6 0.8 copy-start.3
  57.4 1.9 %copy-start.5 = (s32[1,2,1]{1,2,0:T(1,128)S(1)}, s32[1,2,1]{1,2,0:T(1,128)}, u32[]{:S(2)}) copy-start(s32[1,2,1]{1,2,0:T(1,128)} %param.9) | copy-start | bytes 28
  57.5 1.8 %copy-start.4 = (f32[256,512]{1,0:T(8,128)S(1)}, f32[256,512]{1,0:T(8,128)}, u32[]{:S(2)}) copy-start(f32[256,512]{1,0:T(8,128)} %copy-done.3) | copy-start | bytes 1572868
